TPU v7x, 32 devices: a whole 2x2x4 slice. The times are simulated.
32 devices in a mesh: ctx: 8 (over y, x, core), head: 4 (over z).
Axes of the slice: x: 2, y: 2, z: 4, core: 2. Of those that a mesh axis runs over, the one named last changes fastest.
Arguments:
- q_prompt: bfloat16 [4096, 32, 256], P('ctx', 'head'), may hold values from -0.3984375 to 0.3984375
- k_prompt: bfloat16 [4096, 32, 256], P('ctx', 'head'), may hold values from -0.3984375 to 0.3984375
- v_prompt: bfloat16 [4096, 32, 256], P('ctx', 'head'), may hold values from -6 to 6
- log_decay: float32 [32, 4096], P('head', 'ctx'), may hold values from -1 to 0
- prompt_section: int32 [256, 1], P('ctx'), may hold values from 0 to 7; in each aligned block of 32 rows (0 to 31, 32 to 63, ...) at most 4 rows name the same one
- q_step: bfloat16 [256, 4, 32, 256], P('ctx', None, 'head'), may hold values from -0.3984375 to 0.3984375
- k_step: bfloat16 [256, 4, 32, 256], P('ctx', None, 'head'), may hold values from -3 to 3
- v_step: bfloat16 [256, 4, 32, 256], P('ctx', None, 'head'), may hold values from -6 to 6
- step_decay: float32 [32, 4, 256], P('head', None, 'ctx'), may hold values from -0.6 to -0.05
- w_out: bfloat16 [8192, 8192], P(None, 'head'), may hold values from -0.0625 to 0.0625
Outputs:
- prompt_out: bfloat16 [4096, 8192], P('ctx', 'head')
- step_out: bfloat16 [256, 4, 8192], P('ctx', None, 'head')
Inputs may be any that keep to these rules, and one draw needn't show every extreme that they name: `prompt_section`: among the rows of one index of ctx, no section is named more than 4 times.
All inputs are finite; a program needn't handle non-finite values.
Results may differ from a plain program's by a relative error of at most 0.015.
Values may be sent and summed in bfloat16 or wider, within the bound.
A program may use at most 128 MiB of HBM per device.

v0:
```python
import jax
import jax.numpy as jnp
from jax import lax
from jax.sharding import PartitionSpec as P

CAP = 4


def entering(value, axis, join, neutral):
    count, mine = (lax.axis_size(axis), lax.axis_index(axis))
    pieces = jax.tree.map(lambda part: lax.all_gather(part, axis), value)
    running = jax.tree.map(
        lambda part, zero: jnp.full_like(part, 0) + jnp.asarray(zero, part.dtype), value, neutral
    )

    def step(position, running):
        longer = join(running, jax.tree.map(lambda part: part[position], pieces))
        return jax.tree.map(lambda new, old: jnp.where(position < mine, new, old), longer, running)

    return lax.fori_loop(0, count - 1, step, running)


def as_sent(value):
    return jax.tree.map(lambda a: a.astype(jnp.bfloat16) if a.dtype == jnp.float32 else a, value)


def split_state(state):
    high_part = state.astype(jnp.bfloat16)
    rest = state - lax.optimization_barrier(high_part).astype(jnp.float32)
    middle_part = rest.astype(jnp.bfloat16)
    low_part = (rest - lax.optimization_barrier(middle_part).astype(jnp.float32)).astype(
        jnp.bfloat16
    )
    return (high_part, middle_part, low_part)


def exact_read(form, query_rows, state):
    parts = split_state(state)
    total = jnp.einsum(form, query_rows, parts[0], preferred_element_type=jnp.float32)
    total = total + jnp.einsum(form, query_rows, parts[1], preferred_element_type=jnp.float32)
    return total + jnp.einsum(form, query_rows, parts[2], preferred_element_type=jnp.float32)


def block_terms(carry_state, query_rows, key_matrix_rows, value_rows, log_rates):
    positions = jnp.arange(log_rates.shape[1])
    causal = positions[:, None] >= positions[None, :]
    cumlog = jnp.cumsum(log_rates, axis=1)
    decays = jnp.where(
        causal[None], jnp.exp(jnp.minimum(cumlog[:, :, None] - cumlog[:, None, :], 0.0)), 0.0
    )
    attention_scores = jnp.einsum(
        "jsv,csv->sjc", query_rows, key_matrix_rows, preferred_element_type=jnp.float32
    )
    weights = (attention_scores * decays).astype(jnp.bfloat16)
    within = jnp.einsum("hnm,mhe->nhe", weights, value_rows, preferred_element_type=jnp.float32)
    carried = exact_read("nhd,hde->nhe", query_rows, carry_state)
    carried = carried * jnp.exp(cumlog).T[:, :, None]
    last_log = cumlog[:, -1]
    weighted_values = (
        key_matrix_rows.astype(jnp.float32) * jnp.exp(last_log[:, None] - cumlog).T[:, :, None]
    ).astype(jnp.bfloat16)
    state_update = jnp.einsum(
        "jxa,jxp->xap", weighted_values, value_rows, preferred_element_type=jnp.float32
    )
    carry_state = jnp.exp(last_log)[:, None, None] * carry_state + state_update
    return (carry_state, within + carried, cumlog)


def combine(earlier, latter):
    return (earlier[0] + latter[0], jnp.exp(latter[0])[:, None, None] * earlier[1] + latter[1])


def shards(
    q_prompt,
    k_prompt,
    v_prompt,
    log_decay,
    prompt_section,
    q_step,
    k_step,
    v_step,
    step_decay,
    w_out,
):
    token_count, heads_here, head_dim = q_prompt.shape
    sections = lax.axis_size("ctx")
    carry_state = jnp.zeros((heads_here, head_dim, head_dim), jnp.float32)
    carry_state, partial_value, cumlog = block_terms(
        carry_state, q_prompt, k_prompt, v_prompt, log_decay
    )
    offset = cumlog[:, -1]
    identity = (jnp.zeros_like(offset), jnp.zeros_like(carry_state))
    earlier_log, entry_state = entering((offset, carry_state), "ctx", combine, identity)
    entry_parts = split_state(entry_state)
    entry_read = jnp.einsum(
        "nhd,hde->nhe", q_prompt, entry_parts[0], preferred_element_type=jnp.float32
    )
    entry_read = entry_read + jnp.einsum(
        "nhd,hde->nhe", q_prompt, entry_parts[1], preferred_element_type=jnp.float32
    )
    entry_read = entry_read + jnp.einsum(
        "nhd,hde->nhe", q_prompt, entry_parts[2], preferred_element_type=jnp.float32
    )
    block_out = partial_value + jnp.exp(cumlog).T[:, :, None] * entry_read
    retained = block_out.astype(jnp.bfloat16)
    retention = retained.reshape(token_count, heads_here * head_dim)

    def project_into(shard_piece):
        return jnp.dot(shard_piece, w_out, preferred_element_type=jnp.float32)

    prompt_out = project_into(lax.all_gather(retention, "head", axis=1, tiled=True))
    prompt_out = prompt_out.astype(jnp.bfloat16)
    final_state = jnp.exp(offset)[:, None, None] * entry_state + carry_state
    row_count, step_count = (q_step.shape[0], q_step.shape[1])
    section_ids = prompt_section[:, 0]
    owner_hot = (section_ids[:, None] == jnp.arange(sections)[None, :]).astype(jnp.float32)
    before = jnp.tril(jnp.ones((row_count, row_count), jnp.float32), -1)
    counts_before = jnp.dot(before, owner_hot, precision=lax.Precision.HIGHEST)
    ranking = jnp.sum(counts_before * owner_hot, axis=1).astype(jnp.int32)
    slot_ids = section_ids * CAP + ranking
    selector = (jnp.arange(sections * CAP)[:, None] == slot_ids[None, :]).astype(jnp.bfloat16)
    packed = jnp.dot(selector, q_step.reshape(row_count, -1), preferred_element_type=jnp.float32)
    packed = packed.astype(jnp.bfloat16).reshape(sections, CAP, step_count, heads_here, head_dim)
    reads = exact_read(
        "jcthd,jhde->jcthe",
        packed,
        lax.all_gather(as_sent(final_state[None]), "ctx", axis=0, tiled=True),
    )
    slot_reads = reads
    slot_reads = slot_reads.reshape(sections * CAP, step_count, heads_here, head_dim)
    prefix_reads = jnp.take(slot_reads, slot_ids, axis=0)
    step_logs = jnp.cumsum(jnp.transpose(step_decay, (2, 1, 0)), axis=1)
    head_logs = jnp.transpose(step_logs, (0, 2, 1))
    step_index = jnp.arange(step_count)
    causal = step_index[:, None] >= step_index[None, :]
    step_weights = jnp.where(
        causal[None, None],
        jnp.exp(jnp.minimum(head_logs[:, :, :, None] - head_logs[:, :, None, :], 0.0)),
        0.0,
    )
    attention_scores = jnp.einsum(
        "rthd,ruhd->rhtu", q_step, k_step, preferred_element_type=jnp.float32
    )
    own_terms = jnp.einsum(
        "rhtu,ruhe->rthe", attention_scores * step_weights, v_step.astype(jnp.float32)
    )
    step_retention = (jnp.exp(step_logs)[:, :, :, None] * prefix_reads + own_terms).astype(
        jnp.bfloat16
    )
    step_flat = step_retention.reshape(row_count * step_count, heads_here * head_dim)
    step_out = project_into(lax.all_gather(step_flat, "head", axis=1, tiled=True))
    step_out = step_out.astype(jnp.bfloat16).reshape(row_count, step_count, w_out.shape[1])
    return (prompt_out, step_out)


def solution(mesh):
    in_specs = (
        P("ctx", "head", None),
        P("ctx", "head", None),
        P("ctx", "head", None),
        P("head", "ctx"),
        P("ctx", None),
        P("ctx", None, "head", None),
        P("ctx", None, "head", None),
        P("ctx", None, "head", None),
        P("head", None, "ctx"),
        P(None, "head"),
    )
    out_specs = (P("ctx", "head"), P("ctx", None, "head"))
    return jax.shard_map(shards, mesh=mesh, in_specs=in_specs, out_specs=out_specs, check_vma=False)
```

profile of v0, /device:TPU:0, one launch (start us, length us, event | category | flops | bytes accessed | tf_op | source)
XLA Modules:
  0.0 415.0 jit_solution(15389587207151752612)
XLA Ops:
  7.2 2.4 reduce-window.6
  10.3 1.9 multiply_convert_fusion.2
  12.2 2.9 fusion.24
  15.2 0.6 copy-done.9
  15.8 0.6 dynamic-slice
  17.0 0.2 dynamic-update-slice
  17.3 15.2 %all-reduce = f32[64]{0:T(128)S(1)} all-reduce(f32[64]{0:T(128)S(1)} %dynamic-update-slice), channel_id=2, replica_groups=mesh['ctx'=8,'head'=4] {'ctx'}, use_global_device_ids=true, to_apply=%add | all-reduce | flops 64 | bytes 512
  32.5 75.3 %all-gather.12.cloned.1.call-done = f32[64,256,256]{2,1,0:T(8,128)} async-done(((f32[8,256,256]{2,1,0:T(8,128)}), f32[64,256,256]{2,1,0:T(8,128)}) %all-gather.12.cloned.1.call-update) | async-done | bytes 16777232 | tf_op jit(solution)/shard_map/all_gather | solution.py:11
  107.9 26.8 %while.14 = (s32[]{:T(128)}, f32[8,256,256]{2,1,0:T(8,128)}, s32[]{:T(128)}, f32[8,8]{1,0:T(8,128)S(1)}, f32[8,8,256,256]{3,2,1,0:T(8,128)}, /*index=5*/s32[]{:T(128)}, s32[]{:T(128)}) while((s32[]{:T(128)}, f32[8,256,256]{2,1,0:T(8,128)}, s32[]{:T(128)}, f32[8,8]{1,0:T(8,128)S(1)}, f32[8,8,256,256]{3,2,1,0:T(8,128)}, ...), condition=%wide.region_3.4_spmd.clone, body=%wide.region_2.3_spmd.clone.sunk | while | flops 2097156 | bytes 6291657 | solution.py:20
  107.9 3.3 fusion.98
  111.2 3.9 fusion.98
  115.1 3.9 fusion.98
  119.0 3.9 fusion.98
  123.0 3.9 fusion.98
  126.9 3.9 fusion.98
  130.8 3.9 fusion.98
  134.7 4.3 %add_convert_fusion = (bf16[8,256,256]{2,1,0:T(8,128)(2,1)}, bf16[8,256,256]{2,1,0:T(8,128)(2,1)S(1)}) fusion(f32[8,256,256]{2,1,0:T(8,128)} %fusion.24, f32[8,256,256]{2,1,0:T(8,128)} %get-tuple-element.96, f32[8]{0:T(128)S(1)} %get-tuple-element.131), kind=kLoop, calls=%fused_computation.30 | loop fusion | flops 2097152 | bytes 6291488 | tf_op jit(solution)/shard_map/convert_element_type | solution.py:24
  139.0 0.2 all-gather.8.cloned.1.call-start
  139.4 0.2 fusion.21
  139.7 1.2 copy-done.3
  140.9 2.9 fusion.53
  143.8 3.0 fusion.51
  146.8 2.9 fusion.42
  149.7 9.3 %fusion.7 = f32[8,512,256]{1,2,0:T(8,128)} fusion(f32[8,512]{1,0:T(8,128)S(1)} %get-tuple-element.128, pred[512,512]{1,0:T(8,128)(4,1)S(1)} %iota_compare_fusion, bf16[512,8,256]{2,1,0:T(8,128)(2,1)} %param.13, bf16[512,8,256]{2,1,0:T(8,128)(2,1)S(1)} %copy-done, bf16[512,8,256]{2,1,0:T(8,128)(2,1)} %param.12), kind=kOutput, calls=%fused_computation.13 | convolution fusion | flops 2157969408 | bytes 10764288 | tf_op jit(solution)/shard_map/hnm,mhe->nhe/dot_general | solution.py:55
  159.0 2.0 fusion.29
  161.0 0.2 copy-done.4
  161.2 2.9 fusion.46
  164.2 2.9 fusion.48
  167.1 11.8 %fusion.9 = bf16[512,8,256]{0,2,1:T(8,128)(2,1)} fusion(f32[8,512,256]{1,2,0:T(8,128)} %fusion.7, f32[8,256,512]{2,1,0:T(8,128)} %fusion.48, f32[8,256,512]{2,1,0:T(8,128)} %fusion.46, f32[8,256,512]{2,1,0:T(8,128)} %fusion.42, f32[8,256,512]{2,1,0:T(8,128)} %fusion.53, f32[8,256,512]{2,1,0:T(8,128)} %fusion.51, f32[512,8]{0,1:T(8,128)S(1)} %get-tuple-element.127, ...), kind=kOutput, calls=%fused_computation.16 | convolution fusion | flops 548929536 | bytes 33570816 | tf_op jit(solution)/shard_map/nhd,hde->nhe/dot_general | solution.py:101
  179.0 0.3 all-gather.10.cloned.1.call-start
  179.2 0.7 copy-done.5
  180.0 0.3 copy.117
  180.3 0.2 fusion.41
  180.5 0.3 convolution_convert_fusion
  181.3 12.3 %all-gather.14.cloned.1.call-done = bf16[64,256,256]{2,1,0:T(8,128)(2,1)} async-done(((bf16[8,256,256]{2,1,0:T(8,128)(2,1)}), bf16[64,256,256]{2,1,0:T(8,128)(2,1)}) %all-gather.14.cloned.1.call-update) | async-done | bytes 8388624 | tf_op jit(solution)/shard_map/all_gather | solution.py:127
  193.6 13.3 %fusion.1 = bf16[8,8,256,256]{3,2,1,0:T(8,128)(2,1)} fusion(bf16[8,8,256,256]{3,2,1,0:T(8,128)(2,1)} %bitcast.94), kind=kLoop, calls=%fused_computation.6 | loop fusion | flops 16777216 | bytes 16777216 | tf_op jit(solution)/shard_map/convert_element_type | solution.py:30
  206.8 6.3 %fusion.69 = f32[8,8,256,4,4]{2,4,3,1,0:T(4,128)} fusion(bf16[8,8,256,256,1]{3,2,4,1,0:T(8,128)(2,1)} %bitcast.95, bf16[8,4,4,8,256]{4,3,2,1,0:T(8,128)(2,1)S(1)} %bitcast.105), kind=kOutput, calls=%fused_computation.75 | convolution fusion | flops 134217728 | bytes 9961472 | tf_op jit(solution)/shard_map/jcthd,jhde->jcthe/dot_general | solution.py:39
  213.1 12.4 %fusion.5 = f32[8,8,256,4,4]{2,4,3,1,0:T(4,128)} fusion(bf16[8,8,256,256]{3,2,1,0:T(8,128)(2,1)} %fusion.1, bf16[8,8,256,256]{3,2,1,0:T(8,128)(2,1)} %bitcast.96, bf16[8,4,4,8,256]{4,3,2,1,0:T(8,128)(2,1)S(1)} %bitcast.106), kind=kOutput, calls=%fused_computation.12 | convolution fusion | flops 159383552 | bytes 18350080 | tf_op jit(solution)/shard_map/jcthd,jhde->jcthe/dot_general | solution.py:41
  225.6 5.2 %fusion.37 = f32[8,4,4,8,256]{4,2,1,3,0:T(4,128)S(1)} fusion(f32[8,8,256,4,4]{2,4,3,1,0:T(4,128)} %fusion.5, f32[8,8,256,4,4]{2,4,3,1,0:T(4,128)} %fusion.69, bf16[8,8,256,256]{3,2,1,0:T(8,128)(2,1)} %fusion.1, bf16[8,4,4,8,256]{4,3,2,1,0:T(8,128)(2,1)S(1)} %bitcast.107), kind=kOutput, calls=%fused_computation.44 | convolution fusion | flops 134742016 | bytes 12058624 | tf_op jit(solution)/shard_map/jcthd,jhde->jcthe/dot_general | solution.py:40
  230.8 0.6 copy.103
  231.4 0.6 gather_fusion
  232.1 2.2 fusion.40
  234.4 0.9 copy.119
  235.4 110.1 %all-gather.8.cloned.1.call-done = bf16[512,8192]{0,1:T(8,128)(2,1)} async-done(((bf16[512,2048]{0,1:T(8,128)(2,1)}), bf16[512,8192]{0,1:T(8,128)(2,1)}) %all-gather.8.cloned.1.call-update) | async-done | bytes 8388624 | tf_op jit(solution)/shard_map/all_gather | solution.py:111
  345.4 24.6 %convolution_convert_fusion.1 = bf16[512,2048]{1,0:T(8,128)(2,1)} fusion(bf16[512,8192]{0,1:T(8,128)(2,1)} %all-gather.8.cloned.1.call-done, bf16[8192,2048]{1,0:T(8,128)(2,1)} %param.21), kind=kOutput, calls=%fused_computation.24 | convolution fusion | flops 17180917760 | bytes 44040192 | tf_op jit(solution)/shard_map/dot_general | solution.py:109
  370.1 21.5 %all-gather.10.cloned.1.call-done = bf16[128,8192]{1,0:T(8,128)(2,1)} async-done(((bf16[128,2048]{1,0:T(8,128)(2,1)}), bf16[128,8192]{1,0:T(8,128)(2,1)}) %all-gather.10.cloned.1.call-update) | async-done | bytes 2097168 | tf_op jit(solution)/shard_map/all_gather | solution.py:151
  391.6 15.8 %convolution_convert_fusion.2 = bf16[128,2048]{1,0:T(8,128)(2,1)S(1)} fusion(bf16[128,8192]{1,0:T(8,128)(2,1)} %all-gather.10.cloned.1.call-done, bf16[8192,2048]{1,0:T(8,128)(2,1)} %param.21), kind=kOutput, calls=%fused_computation.26 | convolution fusion | flops 4295229440 | bytes 36175872 | tf_op jit(solution)/shard_map/dot_general | solution.py:109
  407.4 1.0 reshape.130
  (53 shorter events, 1.7 us)
Async XLA Ops:
  7.2 5.1 %copy-start = (bf16[512,8,256]{2,1,0:T(8,128)(2,1)S(1)}, bf16[512,8,256]{2,1,0:T(8,128)(2,1)}, u32[]{:S(2)}) copy-start(bf16[512,8,256]{2,1,0:T(8,128)(2,1)} %param.14) | copy-start | bytes 6291460
  7.2 100.7 %all-gather.12.cloned.1.call-start = ((), (), s32[]{:S(2)}) async-start(), calls=%async_computation.2 | async-start | bytes 18874368 | tf_op jit(solution)/shard_map/all_gather | solution.py:11
  15.1 0.7 copy-start.9
  15.1 178.4 %all-gather.14.cloned.1.call-start = ((), (), s32[]{:S(2)}) async-start(), calls=%async_computation.3 | async-start | bytes 9437184 | tf_op jit(solution)/shard_map/all_gather | solution.py:127
  139.0 206.4 %all-gather.8.cloned.1.call-start = ((), (), s32[]{:S(2)}) async-start(), calls=%async_computation | async-start | bytes 10485760 | tf_op jit(solution)/shard_map/all_gather | solution.py:111
  139.3 1.6 copy-start.3
  159.0 2.2 copy-start.4
  164.2 2.9 copy-start.2
  178.9 1.0 copy-start.5
  178.9 1.4 copy-start.7
  179.0 2.0 copy-start.6
  179.0 212.6 %all-gather.10.cloned.1.call-start = ((), (), s32[]{:S(2)}) async-start(), calls=%async_computation.1 | async-start | bytes 2621440 | tf_op jit(solution)/shard_map/all_gather | solution.py:151
  230.8 1.3 copy-start.8
  391.6 16.8 %copy-start.1 = (bf16[512,8,256]{2,1,0:T(8,128)(2,1)S(1)}, bf16[512,8,256]{2,1,0:T(8,128)(2,1)}, u32[]{:S(2)}) copy-start(bf16[512,8,256]{2,1,0:T(8,128)(2,1)} %param.14) | copy-start | bytes 6291460
Sparse Core Ops, SparseCore 0:
  15.3 92.5 all-gather.11
  139.2 54.3 all-gather.13
  195.7 149.6 all-gather.7
  347.4 44.1 all-gather.9
where the time goes:
time: 415 us
  waiting for transfers between devices  219 us (53%)
  matrix products  106 us (26%)
  other arithmetic  51.2 us (12%)
  blocking collectives  15.2 us (4%)
  between operations  14.7 us (4%)
  local copies, waits for them, and re-layouts  8.18 us (2%)
    all_gather x1, waiting for transfers between devices, shards(): lax.all_gather(retention, 'head', axis=1, tiled=True)  110 us
    all_gather x1, waiting for transfers between devices, entering(): pieces = jax.tree.map(lambda part: lax.all_gather(part, axis), value)  75.3 us
    dot_general x2, matrix products, project_into(): return jnp.dot(shard_piece, w_out, preferred_element_type=jnp.float32)  40.5 us
    select_n x7, other arithmetic, step(): jnp.where(position < mine, new, old)  26.8 us
    all_gather x1, waiting for transfers between devices, shards(): lax.all_gather(step_flat, 'head', axis=1, tiled=True)  21.5 us
    convert_element_type x3, other arithmetic, split_state(): middle_part = rest.astype(jnp.bfloat16)  15.4 us
    dot_general x2, matrix products, exact_read(): jnp.einsum(form, query_rows, parts[2], preferred_element_type=jnp.float32)  15.4 us
    unnamed x1, blocking collectives  15.2 us
  transfers between devices with their start and end apart: 4, of which 4 were waited for; matrix products, arithmetic and copies ran while one was open for 26% of the time, Pallas kernels for 0%

commit v1 on v0

--- a/solution.py
+++ b/solution.py
@@ -1,9 +1,352 @@
+import functools
 import jax
 import jax.numpy as jnp
 from jax import lax
+from jax.experimental import pallas as pl
+from jax.experimental.pallas import tpu as pltpu
 from jax.sharding import PartitionSpec as P
 
 CAP = 4
+MESH = pl.DeviceIdType.MESH
+F32 = jnp.float32
+BF16 = jnp.bfloat16
+
+
+def mm(a, b):
+    return jnp.dot(a, b, preferred_element_type=F32)
+
+
+def retention_kernel(
+    sections,
+    q_ref, k_ref, v_ref, cum_ref, cum_t_ref, total_ref,
+    qs_ref, ks_ref, vs_ref, step_log_ref, pack_ref, unpack_ref,
+    out_ref,
+    state_out, query_out, state_in, query_in, total_in,
+    boundary, entry_out, read_out, entry_in, read_in, within, own,
+    send_s, send_a, send_q, send_e, send_r,
+    recv_s, recv_a, recv_q, recv_e, recv_r,
+):
+    me = lax.axis_index("ctx")
+    heads = total_ref.shape[0]
+    tokens = q_ref.shape[0]
+    hd = q_ref.shape[1] // heads
+    rows = step_log_ref.shape[0]
+    steps = qs_ref.shape[0] // rows
+
+    def peer(d):
+        return lax.rem(me + d, sections)
+
+    def push(src, dst, send, recv, to):
+        return pltpu.make_async_remote_copy(
+            src_ref=src, dst_ref=dst, send_sem=send, recv_sem=recv,
+            device_id={"ctx": to}, device_id_type=MESH,
+        )
+
+    barrier = pltpu.get_barrier_semaphore()
+    for d in range(1, sections):
+        pl.semaphore_signal(barrier, inc=1, device_id={"ctx": peer(d)}, device_id_type=MESH)
+
+    def lanes(h):
+        return slice(h * hd, (h + 1) * hd)
+
+    for h in range(heads):
+        column = cum_t_ref[:, h:h + 1]
+        keys = (k_ref[:, lanes(h)].astype(F32) * jnp.exp(total_ref[h, 0:1, 0:1] - column)).astype(BF16)
+        state_out[h] = lax.dot_general(
+            keys, v_ref[:, lanes(h)], (((0,), (0,)), ((), ())), preferred_element_type=F32
+        ).astype(BF16)
+    pl.semaphore_wait(barrier, sections - 1)
+    for d in range(1, sections):
+        to = peer(d)
+        push(total_ref.at[to], total_in.at[me], send_a.at[d], recv_a.at[me], to).start()
+        push(state_out.at[to], state_in.at[me], send_s.at[d], recv_s.at[me], to).start()
+    state_in[me] = state_out[me]
+    total_in[me] = total_ref[me]
+    for h in range(heads):
+        query_out[h] = mm(pack_ref[...], qs_ref[:, lanes(h)]).astype(BF16)
+    for d in range(1, sections):
+        to = peer(d)
+        push(query_out.at[to], query_in.at[me], send_q.at[d], recv_q.at[me], to).start()
+    query_in[me] = query_out[me]
+
+    causal = (
+        lax.broadcasted_iota(jnp.int32, (tokens, tokens), 0)
+        >= lax.broadcasted_iota(jnp.int32, (tokens, tokens), 1)
+    )
+    for h in range(heads):
+        scores = lax.dot_general(
+            q_ref[:, lanes(h)], k_ref[:, lanes(h)], (((1,), (1,)), ((), ())),
+            preferred_element_type=F32,
+        )
+        gap = jnp.minimum(cum_t_ref[:, h:h + 1] - cum_ref[h:h + 1, :], 0.0)
+        weights = jnp.where(causal, scores * jnp.exp(gap), 0.0).astype(BF16)
+        within[:, lanes(h)] = mm(weights, v_ref[:, lanes(h)])
+
+    for h in range(heads):
+        for t in range(steps):
+            here = slice(t * rows, (t + 1) * rows)
+            query = qs_ref[here, lanes(h)].astype(F32)
+            log_t = step_log_ref[:, t * heads + h:t * heads + h + 1]
+            acc = jnp.zeros((rows, hd), F32)
+            for u in range(t + 1):
+                there = slice(u * rows, (u + 1) * rows)
+                score = jnp.sum(query * ks_ref[there, lanes(h)].astype(F32), axis=1, keepdims=True)
+                log_u = step_log_ref[:, u * heads + h:u * heads + h + 1]
+                weight = score * jnp.exp(jnp.minimum(log_t - log_u, 0.0))
+                acc = acc + weight * vs_ref[there, lanes(h)].astype(F32)
+            own[here, lanes(h)] = acc
+
+    for d in range(1, sections):
+        frm = peer(d)
+        push(total_ref.at[frm], total_in.at[frm], send_a.at[d], recv_a.at[frm], frm).wait_recv()
+        push(state_out.at[frm], state_in.at[frm], send_s.at[d], recv_s.at[frm], frm).wait_recv()
+    state = jnp.zeros((hd, hd), F32)
+    for c in range(sections):
+        entry_out[c] = state.astype(BF16)
+        state = jnp.exp(total_in[c, 0:1, 0:1]) * state + state_in[c].astype(F32)
+        boundary[c] = state.astype(BF16)
+    for d in range(1, sections):
+        to = peer(d)
+        push(entry_out.at[to], entry_in.at[me], send_e.at[d], recv_e.at[me], to).start()
+    entry_in[me] = entry_out[me]
+
+    for d in range(1, sections):
+        frm = peer(d)
+        push(query_out.at[frm], query_in.at[frm], send_q.at[d], recv_q.at[frm], frm).wait_recv()
+    span = CAP * steps
+    for c in range(sections):
+        part = slice(c * span, (c + 1) * span)
+        asked = query_in[:, part, :].reshape(sections * span, hd)
+        read_out[:, part, :] = mm(asked, boundary[c]).astype(BF16).reshape(sections, span, hd)
+    for d in range(1, sections):
+        to = peer(d)
+        push(read_out.at[to], read_in.at[me], send_r.at[d], recv_r.at[me], to).start()
+    read_in[me] = read_out[me]
+
+    for d in range(1, sections):
+        frm = peer(d)
+        push(entry_out.at[frm], entry_in.at[frm], send_e.at[d], recv_e.at[frm], frm).wait_recv()
+    for h in range(heads):
+        carried = mm(q_ref[:, lanes(h)], entry_in[h]) * jnp.exp(cum_t_ref[:, h:h + 1])
+        out_ref[0:tokens, lanes(h)] = (within[:, lanes(h)] + carried).astype(BF16)
+
+    for d in range(1, sections):
+        frm = peer(d)
+        push(read_out.at[frm], read_in.at[frm], send_r.at[d], recv_r.at[frm], frm).wait_recv()
+    for h in range(heads):
+        reads = mm(unpack_ref[...], read_in[h])
+        for t in range(steps):
+            here = slice(t * rows, (t + 1) * rows)
+            grown = jnp.exp(step_log_ref[:, t * heads + h:t * heads + h + 1])
+            out_ref[tokens + t * rows:tokens + (t + 1) * rows, lanes(h)] = (
+                grown * reads[here] + own[here, lanes(h)]
+            ).astype(BF16)
+
+    for d in range(1, sections):
+        to = peer(d)
+        push(total_ref.at[to], total_in.at[me], send_a.at[d], recv_a.at[me], to).wait_send()
+        push(state_out.at[to], state_in.at[me], send_s.at[d], recv_s.at[me], to).wait_send()
+        push(query_out.at[to], query_in.at[me], send_q.at[d], recv_q.at[me], to).wait_send()
+        push(entry_out.at[to], entry_in.at[me], send_e.at[d], recv_e.at[me], to).wait_send()
+        push(read_out.at[to], read_in.at[me], send_r.at[d], recv_r.at[me], to).wait_send()
+
+
+def project_kernel(
+    n, r_ref, w_ref, out_ref, gathered, weights, total, load_sem, send_sem, recv_sem
+):
+    at = lax.axis_index("head")
+    chunks, _, depth = r_ref.shape
+    columns = w_ref.shape[1]
+    tile = min(columns, 512)
+
+    def load(j):
+        return pltpu.make_async_copy(
+            w_ref.at[pl.ds(pl.multiple_of(j * depth, depth), depth)], weights.at[j], load_sem.at[j]
+        )
+
+    def push(src, j, m, way, s):
+        return pltpu.make_async_remote_copy(
+            src_ref=src, dst_ref=gathered.at[j, m],
+            send_sem=send_sem.at[way, s, m], recv_sem=recv_sem.at[j, m],
+            device_id={"head": at + 1 if way == 0 else at - 1}, device_id_type=MESH,
+        )
+
+    has_left, has_right = at > 0, at < n - 1
+    barrier = pltpu.get_barrier_semaphore()
+
+    @pl.when(has_left)
+    def _():
+        pl.semaphore_signal(barrier, inc=1, device_id={"head": at - 1}, device_id_type=MESH)
+
+    @pl.when(has_right)
+    def _():
+        pl.semaphore_signal(barrier, inc=1, device_id={"head": at + 1}, device_id_type=MESH)
+
+    pl.semaphore_wait(barrier, has_left.astype(jnp.int32) + has_right.astype(jnp.int32))
+
+    for m in range(chunks):
+        @pl.when(has_right)
+        def _():
+            push(r_ref.at[m], at, m, 0, 0).start()
+
+        @pl.when(has_left)
+        def _():
+            push(r_ref.at[m], at, m, 1, 0).start()
+
+    for j in range(n):
+        load(j).start()
+
+    def multiply(rows, j, m, first):
+        def body(i, carry):
+            cols = pl.ds(pl.multiple_of(i * tile, tile), tile)
+            term = mm(rows[...], weights[j, :, cols])
+            if first:
+                total[m, :, cols] = term
+            else:
+                total[m, :, cols] += term
+            return carry
+
+        lax.fori_loop(0, columns // tile, body, 0)
+
+    for j in range(n):
+        load(j).wait()
+
+    def own_step(m, carry):
+        multiply(r_ref.at[m], at, m, True)
+        return carry
+
+    lax.fori_loop(0, chunks, own_step, 0)
+
+    def step(i, carry):
+        s, m = i // chunks + 1, lax.rem(i, chunks)
+        low, high = at - s, at + s
+
+        @pl.when(low >= 0)
+        def _():
+            push(gathered.at[low, m], low, m, 0, s).wait_recv()
+
+            @pl.when(has_right)
+            def _():
+                push(gathered.at[low, m], low, m, 0, s).start()
+
+        @pl.when(high < n)
+        def _():
+            push(gathered.at[high, m], high, m, 1, s).wait_recv()
+
+            @pl.when(has_left)
+            def _():
+                push(gathered.at[high, m], high, m, 1, s).start()
+
+        @pl.when(low >= 0)
+        def _():
+            multiply(gathered.at[low, m], low, m, False)
+
+        @pl.when(high < n)
+        def _():
+            multiply(gathered.at[high, m], high, m, False)
+
+        return carry
+
+    lax.fori_loop(0, (n - 1) * chunks, step, 0)
+
+    def finish(m, carry):
+        out_ref[m] = total[m].astype(BF16)
+        return carry
+
+    lax.fori_loop(0, chunks, finish, 0)
+
+    def drain(i, carry):
+        s, m = i // chunks, lax.rem(i, chunks)
+
+        @pl.when((at - s >= 0) & has_right)
+        def _():
+            push(r_ref.at[m], at - s, m, 0, s).wait_send()
+
+        @pl.when((at + s < n) & has_left)
+        def _():
+            push(r_ref.at[m], at + s, m, 1, s).wait_send()
+
+        return carry
+
+    lax.fori_loop(0, n * chunks, drain, 0)
+
+
+def project(flat, w_out):
+    n = lax.axis_size("head")
+    chunk = 128
+    chunks, depth = flat.shape[0] // chunk, flat.shape[1]
+    columns = w_out.shape[1]
+    vmem = pl.BlockSpec(memory_space=pltpu.VMEM)
+    out = pl.pallas_call(
+        functools.partial(project_kernel, n),
+        out_shape=jax.ShapeDtypeStruct((chunks, chunk, columns), BF16),
+        in_specs=[vmem, pl.BlockSpec(memory_space=pl.ANY)],
+        out_specs=vmem,
+        scratch_shapes=[
+            pltpu.VMEM((n, chunks, chunk, depth), BF16),
+            pltpu.VMEM((n, depth, columns), BF16),
+            pltpu.VMEM((chunks, chunk, columns), F32),
+            pltpu.SemaphoreType.DMA((n,)),
+            pltpu.SemaphoreType.DMA((2, n, chunks)),
+            pltpu.SemaphoreType.DMA((n, chunks)),
+        ],
+        compiler_params=pltpu.CompilerParams(
+            collective_id=1, has_side_effects=True, vmem_limit_bytes=60 * 2**20
+        ),
+        name="project",
+    )(flat.reshape(chunks, chunk, depth), w_out)
+    return out.reshape(chunks * chunk, columns)
+
+
+def retain(q, k, v, log_decay, prompt_section, q_step, k_step, v_step, step_decay):
+    tokens, heads, hd = q.shape
+    rows, steps = q_step.shape[:2]
+    sections = lax.axis_size("ctx")
+    cumlog = jnp.cumsum(log_decay, axis=1)
+    totals = jnp.broadcast_to(cumlog[:, -1][:, None, None], (heads, 8, 128))
+    section_ids = prompt_section[:, 0]
+    same = section_ids[:, None] == section_ids[None, :]
+    ranking = jnp.sum(jnp.where(jnp.tril(same, -1), 1, 0), axis=1)
+    slot = (jnp.arange(sections)[:, None, None] * CAP + jnp.arange(CAP)[None, None, :])
+    slot = jnp.broadcast_to(slot, (sections, steps, CAP)).reshape(-1)
+    slot_step = jnp.broadcast_to(jnp.arange(steps)[None, :, None], (sections, steps, CAP)).reshape(-1)
+    row_slot = jnp.tile(section_ids * CAP + ranking, steps)
+    row_step = jnp.repeat(jnp.arange(steps), rows)
+    pack = (slot[:, None] == row_slot[None, :]) & (slot_step[:, None] == row_step[None, :])
+    unpack = (row_slot[:, None] == slot[None, :]) & (row_step[:, None] == slot_step[None, :])
+    step_logs = jnp.cumsum(step_decay, axis=1)
+    step_logs = jnp.transpose(step_logs, (2, 1, 0)).reshape(rows, steps * heads)
+
+    def wide(a):
+        return a.reshape(tokens, heads * hd)
+
+    def by_step(a):
+        return jnp.transpose(a, (1, 0, 2, 3)).reshape(steps * rows, heads * hd)
+
+    vmem = pl.BlockSpec(memory_space=pltpu.VMEM)
+    count = sections * CAP * steps
+    state = pltpu.VMEM((sections, hd, hd), BF16)
+    reads = pltpu.VMEM((sections, count, hd), BF16)
+    return pl.pallas_call(
+        functools.partial(retention_kernel, sections),
+        out_shape=jax.ShapeDtypeStruct((tokens + rows * steps, heads * hd), BF16),
+        in_specs=[vmem] * 12,
+        out_specs=vmem,
+        scratch_shapes=[
+            state, reads, state, reads, pltpu.VMEM((sections, 8, 128), F32),
+            state, state, reads, state, reads,
+            pltpu.VMEM((tokens, heads * hd), F32),
+            pltpu.VMEM((rows * steps, heads * hd), F32),
+        ] + [pltpu.SemaphoreType.DMA((sections,))] * 10,
+        compiler_params=pltpu.CompilerParams(
+            collective_id=0, has_side_effects=True, vmem_limit_bytes=48 * 2**20
+        ),
+        name="retain",
+    )(
+        wide(q), wide(k), wide(v), cumlog, cumlog.T, totals,
+        by_step(q_step), by_step(k_step), by_step(v_step), step_logs,
+        pack.astype(BF16), unpack.astype(BF16),
+    )
 
 
 def entering(value, axis, join, neutral):
@@ -70,17 +413,8 @@
     return (earlier[0] + latter[0], jnp.exp(latter[0])[:, None, None] * earlier[1] + latter[1])
 
 
-def shards(
-    q_prompt,
-    k_prompt,
-    v_prompt,
-    log_decay,
-    prompt_section,
-    q_step,
-    k_step,
-    v_step,
-    step_decay,
-    w_out,
+def retain_gathered(
+    q_prompt, k_prompt, v_prompt, log_decay, prompt_section, q_step, k_step, v_step, step_decay
 ):
     token_count, heads_here, head_dim = q_prompt.shape
     sections = lax.axis_size("ctx")
@@ -105,11 +439,6 @@
     retained = block_out.astype(jnp.bfloat16)
     retention = retained.reshape(token_count, heads_here * head_dim)
 
-    def project_into(shard_piece):
-        return jnp.dot(shard_piece, w_out, preferred_element_type=jnp.float32)
-
-    prompt_out = project_into(lax.all_gather(retention, "head", axis=1, tiled=True))
-    prompt_out = prompt_out.astype(jnp.bfloat16)
     final_state = jnp.exp(offset)[:, None, None] * entry_state + carry_state
     row_count, step_count = (q_step.shape[0], q_step.shape[1])
     section_ids = prompt_section[:, 0]
@@ -147,10 +476,32 @@
     step_retention = (jnp.exp(step_logs)[:, :, :, None] * prefix_reads + own_terms).astype(
         jnp.bfloat16
     )
-    step_flat = step_retention.reshape(row_count * step_count, heads_here * head_dim)
-    step_out = project_into(lax.all_gather(step_flat, "head", axis=1, tiled=True))
-    step_out = step_out.astype(jnp.bfloat16).reshape(row_count, step_count, w_out.shape[1])
-    return (prompt_out, step_out)
+    step_flat = jnp.transpose(step_retention, (1, 0, 2, 3))
+    step_flat = step_flat.reshape(row_count * step_count, heads_here * head_dim)
+    return jnp.concatenate([retention, step_flat], axis=0)
+
+
+def shards(
+    q_prompt,
+    k_prompt,
+    v_prompt,
+    log_decay,
+    prompt_section,
+    q_step,
+    k_step,
+    v_step,
+    step_decay,
+    w_out,
+):
+    tokens, heads = q_prompt.shape[:2]
+    rows, steps = q_step.shape[:2]
+    form = retain if heads == lax.axis_size("ctx") else retain_gathered
+    flat = form(
+        q_prompt, k_prompt, v_prompt, log_decay, prompt_section, q_step, k_step, v_step, step_decay
+    )
+    out = project(flat, w_out)
+    step_out = out[tokens:].reshape(steps, rows, w_out.shape[1])
+    return (out[:tokens], jnp.transpose(step_out, (1, 0, 2)))
 
 
 def solution(mesh):

time: 415 us -> 242 us (0.58)
  Pallas kernels: 0 us -> 223 us
  waiting for transfers between devices: 219 us -> 0 us
  matrix products: 106 us -> 0 us
  other arithmetic: 51.2 us -> 4.85 us
  blocking collectives: 15.2 us -> 0 us
  between operations: 14.7 us -> 0.8 us
  local copies, waits for them, and re-layouts: 8.18 us -> 13.3 us
    pallas_call x0 -> x2, Pallas kernels: none -> 223 us  [the longest x1 179 us: project(): pl.pallas_call(functools.partial(project_kernel, n), out_shape=jax.ShapeD...]
    all_gather x4 -> x0, waiting for transfers between devices: 219 us -> none  [the longest x1 110 us: shards(): lax.all_gather(retention, 'head', axis=1, tiled=True)]
    dot_general x16 -> x0, matrix products: 106 us -> none  [the longest x2 40.5 us: project_into(): return jnp.dot(shard_piece, w_out, preferred_element_type=jnp.float32)]
    select_n x7 -> x0, other arithmetic: 26.8 us -> none  [step(): jnp.where(position < mine, new, old)]
    convert_element_type x5 -> x1, other arithmetic: 21.7 us -> 0.14 us  [retain(): unpack.astype(BF16)]
    unnamed x1 -> x0, blocking collectives: 15.2 us -> none
  transfers between devices with their start and end apart: 4 -> 0, of which waited for: 4 -> 0; matrix products, arithmetic and copies ran while one was open for 26% -> 0% of each run, Pallas kernels for 0% -> 0%
where the time goes in v1:
time: 242 us
  Pallas kernels  223 us (92%)
  local copies, waits for them, and re-layouts  13.3 us (5%)
  other arithmetic  4.85 us (2%)
    pallas_call x1, Pallas kernels, project(): pl.pallas_call(functools.partial(project_kernel, n), out_shape=jax.ShapeD...  179 us
    pallas_call x1, Pallas kernels, retain(): pl.pallas_call(functools.partial(retention_kernel, sections), out_shape=j...  43.5 us
    unnamed x16, local copies, waits for them, and re-layouts  6.76 us

profile of v1, /device:TPU:0, one launch (start us, length us, event | category | flops | bytes accessed | tf_op | source)
XLA Modules:
  0.0 241.6 jit_solution(7771654853987327405)
XLA Ops:
  0.6 0.0 copy-start.3
  0.7 0.9 select_reduce_fusion
  1.6 0.7 multiply_add_fusion
  2.2 0.1 eq.84
  2.3 0.1 eq.89
  2.4 0.1 iota_add_fusion
  2.5 0.1 eq.79
  2.6 2.2 reduce-window.6
  4.8 0.2 slice_reduce_fusion
  5.0 0.1 broadcast_add_fusion
  5.1 0.7 reduce-window_bitcast_fusion
  5.8 0.1 copy.33.step_log_ref
  5.9 0.1 eq.87
  6.0 0.1 and_convert_fusion
  6.2 0.1 copy.27
  6.3 0.1 copy.32.cum_ref
  6.4 0.1 broadcast_in_dim.42.total_ref
  6.5 0.0 copy-start.4
  6.5 1.2 copy.28
  7.6 0.1 copy.38
  7.8 0.0 copy-done.3
  7.8 0.0 copy-start
  7.8 0.1 copy.39
  7.9 0.0 copy-done.4
  8.0 0.1 copy.40
  8.1 1.2 copy-done
  9.4 0.0 copy-start.1
  9.4 0.7 copy.35
  10.0 0.9 copy-done.1
  11.0 0.0 copy-start.2
  11.0 0.7 copy.36
  11.6 0.9 copy-done.2
  12.5 2.0 copy.37
  14.5 43.5 %retain.1 = bf16[640,2048]{1,0:T(8,128)(2,1)} custom-call(bf16[512,2048]{1,0:T(8,128)(2,1)S(1)} %bitcast.36, bf16[512,2048]{1,0:T(8,128)(2,1)S(1)} %bitcast.37, bf16[512,2048]{1,0:T(8,128)(2,1)} %bitcast.46, f32[8,512]{1,0:T(8,128)S(1)} %copy.32.cum_ref, f32[512,8]{1,0:T(8,128)S(1)} %bitcast.40, f32[8,8,128]{2,1,0:T(8,128)S(1)} %broadcast_in_dim.42.total_ref, ...), custom_call_target="tpu_custom_call" | custom-call | tf_op jit(solution)/shard_map/retain/pallas_call | solution.py:330
  58.0 179.2 %project.1 = bf16[5,128,2048]{2,1,0:T(8,128)(2,1)} custom-call(bf16[5,128,2048]{2,1,0:T(8,128)(2,1)} %bitcast.45, bf16[8192,2048]{1,0:T(8,128)(2,1)} %w_ref.1), custom_call_target="tpu_custom_call" | custom-call | tf_op jit(solution)/shard_map/project/pallas_call | solution.py:280
  237.2 0.0 slice-start
  237.2 3.2 %slice.22 = bf16[4,128,2048]{2,1,0:T(8,128)(2,1)} slice(bf16[5,128,2048]{2,1,0:T(8,128)(2,1)} %project.1), slice={[0:4], [0:128], [0:2048]} | slice | bytes 4194304 | tf_op jit(solution)/shard_map/slice | solution.py:504
  240.4 0.0 slice-done
  240.4 1.2 copy.44
  (11 shorter events, 0.1 us)
Async XLA Ops:
  0.6 7.1 %copy-start.3 = (bf16[32,4,8,256]{3,2,1,0:T(8,128)(2,1)S(1)}, bf16[32,4,8,256]{3,2,1,0:T(8,128)(2,1)}, u32[]{:S(2)}) copy-start(bf16[32,4,8,256]{3,2,1,0:T(8,128)(2,1)} %param.16) | copy-start | bytes 1572868
  6.5 1.5 copy-start.4
  7.8 1.6 copy-start
  9.4 1.6 copy-start.1
  11.0 1.6 copy-start.2
  237.2 3.2 %slice-start = ((bf16[5,128,2048]{2,1,0:T(8,128)(2,1)}), bf16[1,128,2048]{2,1,0:T(8,128)(2,1)S(1)}, s32[]{:S(2)}) async-start(bf16[5,128,2048]{2,1,0:T(8,128)(2,1)} %project.1), calls=%async_computation | async-start | bytes 1048576 | tf_op jit(solution)/shard_map/slice | solution.py:503

commit v2 on v1

--- a/solution.py
+++ b/solution.py
@@ -16,17 +16,52 @@
     return jnp.dot(a, b, preferred_element_type=F32)
 
 
-def retention_kernel(
+def fused_kernel(
     sections,
     q_ref, k_ref, v_ref, cum_ref, cum_t_ref, total_ref,
     qs_ref, ks_ref, vs_ref, step_log_ref, pack_ref, unpack_ref,
-    out_ref,
+    w_ref,
+    prompt_ref, step_ref,
     state_out, query_out, state_in, query_in, total_in,
-    boundary, entry_out, read_out, entry_in, read_in, within, own,
+    boundary, entry_out, read_out, entry_in, read_in, gathered, weights, total,
     send_s, send_a, send_q, send_e, send_r,
     recv_s, recv_a, recv_q, recv_e, recv_r,
+    load_sem, send_z, recv_z,
 ):
     me = lax.axis_index("ctx")
+    at = lax.axis_index("head")
+    n = lax.axis_size("head")
+    has_left, has_right = at > 0, at < n - 1
+    chunks, chunk, depth = total.shape
+    parts = chunks - 1
+    tile = 512
+    far = jnp.where(at < 2, 3, 0)
+    near = jnp.where(at == 1, 0, 1)
+
+    def slot_of(j):
+        return jnp.where((j == at) | (j == far), 0, jnp.where(j == near, 1, 2))
+
+    def load(j, sem):
+        return pltpu.make_async_copy(
+            w_ref.at[pl.ds(pl.multiple_of(j * depth, depth), depth)],
+            weights.at[slot_of(j)], load_sem.at[sem],
+        )
+
+    def pass_on(j, m, way, s):
+        return pltpu.make_async_remote_copy(
+            src_ref=gathered.at[j, m], dst_ref=gathered.at[j, m],
+            send_sem=send_z.at[way, s, m], recv_sem=recv_z.at[j, m],
+            device_id={"head": at + 1 if way == 0 else at - 1}, device_id_type=MESH,
+        )
+
+    def send_own(m):
+        @pl.when(has_right)
+        def _():
+            pass_on(at, m, 0, 0).start()
+
+        @pl.when(has_left)
+        def _():
+            pass_on(at, m, 1, 0).start()
     heads = total_ref.shape[0]
     tokens = q_ref.shape[0]
     hd = q_ref.shape[1] // heads
@@ -45,6 +80,19 @@
     barrier = pltpu.get_barrier_semaphore()
     for d in range(1, sections):
         pl.semaphore_signal(barrier, inc=1, device_id={"ctx": peer(d)}, device_id_type=MESH)
+
+    @pl.when(has_left)
+    def _():
+        pl.semaphore_signal(barrier, inc=1, device_id={"head": at - 1}, device_id_type=MESH)
+
+    @pl.when(has_right)
+    def _():
+        pl.semaphore_signal(barrier, inc=1, device_id={"head": at + 1}, device_id_type=MESH)
+
+    other = jnp.where(at == 1, 2, jnp.where(at == 2, 3, 2))
+    load(at, 0).start()
+    load(near, 1).start()
+    load(other, 2).start()
 
     def lanes(h):
         return slice(h * hd, (h + 1) * hd)
@@ -55,7 +103,9 @@
         state_out[h] = lax.dot_general(
             keys, v_ref[:, lanes(h)], (((0,), (0,)), ((), ())), preferred_element_type=F32
         ).astype(BF16)
-    pl.semaphore_wait(barrier, sections - 1)
+    pl.semaphore_wait(
+        barrier, sections - 1 + has_left.astype(jnp.int32) + has_right.astype(jnp.int32)
+    )
     for d in range(1, sections):
         to = peer(d)
         push(total_ref.at[to], total_in.at[me], send_a.at[d], recv_a.at[me], to).start()
@@ -79,8 +129,35 @@
             preferred_element_type=F32,
         )
         gap = jnp.minimum(cum_t_ref[:, h:h + 1] - cum_ref[h:h + 1, :], 0.0)
-        weights = jnp.where(causal, scores * jnp.exp(gap), 0.0).astype(BF16)
-        within[:, lanes(h)] = mm(weights, v_ref[:, lanes(h)])
+        scaled = jnp.where(causal, scores * jnp.exp(gap), 0.0).astype(BF16)
+        total[0:parts, :, lanes(h)] = mm(scaled, v_ref[:, lanes(h)]).reshape(parts, chunk, hd)
+
+    for d in range(1, sections):
+        frm = peer(d)
+        push(total_ref.at[frm], total_in.at[frm], send_a.at[d], recv_a.at[frm], frm).wait_recv()
+        push(state_out.at[frm], state_in.at[frm], send_s.at[d], recv_s.at[frm], frm).wait_recv()
+    state = jnp.zeros((hd, hd), F32)
+    for c in range(sections):
+        entry_out[c] = state.astype(BF16)
+        state = jnp.exp(total_in[c, 0:1, 0:1]) * state + state_in[c].astype(F32)
+        boundary[c] = state.astype(BF16)
+    for d in range(1, sections):
+        to = peer(d)
+        push(entry_out.at[to], entry_in.at[me], send_e.at[d], recv_e.at[me], to).start()
+    entry_in[me] = entry_out[me]
+
+    for d in range(1, sections):
+        frm = peer(d)
+        push(query_out.at[frm], query_in.at[frm], send_q.at[d], recv_q.at[frm], frm).wait_recv()
+    span = CAP * steps
+    for c in range(sections):
+        part = slice(c * span, (c + 1) * span)
+        asked = query_in[:, part, :].reshape(sections * span, hd)
+        read_out[:, part, :] = mm(asked, boundary[c]).astype(BF16).reshape(sections, span, hd)
+    for d in range(1, sections):
+        to = peer(d)
+        push(read_out.at[to], read_in.at[me], send_r.at[d], recv_r.at[me], to).start()
+    read_in[me] = read_out[me]
 
     for h in range(heads):
         for t in range(steps):
@@ -94,41 +171,17 @@
                 log_u = step_log_ref[:, u * heads + h:u * heads + h + 1]
                 weight = score * jnp.exp(jnp.minimum(log_t - log_u, 0.0))
                 acc = acc + weight * vs_ref[there, lanes(h)].astype(F32)
-            own[here, lanes(h)] = acc
-
-    for d in range(1, sections):
-        frm = peer(d)
-        push(total_ref.at[frm], total_in.at[frm], send_a.at[d], recv_a.at[frm], frm).wait_recv()
-        push(state_out.at[frm], state_in.at[frm], send_s.at[d], recv_s.at[frm], frm).wait_recv()
-    state = jnp.zeros((hd, hd), F32)
-    for c in range(sections):
-        entry_out[c] = state.astype(BF16)
-        state = jnp.exp(total_in[c, 0:1, 0:1]) * state + state_in[c].astype(F32)
-        boundary[c] = state.astype(BF16)
-    for d in range(1, sections):
-        to = peer(d)
-        push(entry_out.at[to], entry_in.at[me], send_e.at[d], recv_e.at[me], to).start()
-    entry_in[me] = entry_out[me]
-
-    for d in range(1, sections):
-        frm = peer(d)
-        push(query_out.at[frm], query_in.at[frm], send_q.at[d], recv_q.at[frm], frm).wait_recv()
-    span = CAP * steps
-    for c in range(sections):
-        part = slice(c * span, (c + 1) * span)
-        asked = query_in[:, part, :].reshape(sections * span, hd)
-        read_out[:, part, :] = mm(asked, boundary[c]).astype(BF16).reshape(sections, span, hd)
-    for d in range(1, sections):
-        to = peer(d)
-        push(read_out.at[to], read_in.at[me], send_r.at[d], recv_r.at[me], to).start()
-    read_in[me] = read_out[me]
+            total[parts, here, lanes(h)] = acc
 
     for d in range(1, sections):
         frm = peer(d)
         push(entry_out.at[frm], entry_in.at[frm], send_e.at[d], recv_e.at[frm], frm).wait_recv()
-    for h in range(heads):
-        carried = mm(q_ref[:, lanes(h)], entry_in[h]) * jnp.exp(cum_t_ref[:, h:h + 1])
-        out_ref[0:tokens, lanes(h)] = (within[:, lanes(h)] + carried).astype(BF16)
+    for m in range(parts):
+        here = slice(m * chunk, (m + 1) * chunk)
+        for h in range(heads):
+            carried = mm(q_ref[here, lanes(h)], entry_in[h]) * jnp.exp(cum_t_ref[here, h:h + 1])
+            gathered[at, m, :, lanes(h)] = (total[m, :, lanes(h)] + carried).astype(BF16)
+        send_own(m)
 
     for d in range(1, sections):
         frm = peer(d)
@@ -138,9 +191,96 @@
         for t in range(steps):
             here = slice(t * rows, (t + 1) * rows)
             grown = jnp.exp(step_log_ref[:, t * heads + h:t * heads + h + 1])
-            out_ref[tokens + t * rows:tokens + (t + 1) * rows, lanes(h)] = (
-                grown * reads[here] + own[here, lanes(h)]
+            gathered[at, parts, here, lanes(h)] = (
+                grown * reads[here] + total[parts, here, lanes(h)]
             ).astype(BF16)
+    send_own(parts)
+
+    def multiply(j, m, first):
+        slot = slot_of(j)
+
+        def body(i, carry):
+            cols = pl.ds(pl.multiple_of(i * tile, tile), tile)
+            term = mm(gathered[j, m], weights[slot, :, cols])
+            if first:
+                total[m, :, cols] = term
+                return carry
+
+            @pl.when(j != far)
+            def _():
+                total[m, :, cols] += term
+
+            @pl.when((j == far) & (m < parts))
+            def _():
+                here = pl.ds(pl.multiple_of(jnp.minimum(m, parts - 1) * chunk, chunk), chunk)
+                prompt_ref[here, cols] = (total[m, :, cols] + term).astype(BF16)
+
+            @pl.when((j == far) & (m == parts))
+            def _():
+                step_ref[:, cols] = (total[m, :, cols] + term).astype(BF16)
+
+            return carry
+
+        lax.fori_loop(0, depth // tile, body, 0)
+
+    load(at, 0).wait()
+
+    def own_step(m, carry):
+        multiply(at, m, True)
+        return carry
+
+    lax.fori_loop(0, chunks, own_step, 0)
+    load(far, 3).start()
+    load(near, 1).wait()
+    load(other, 2).wait()
+    load(far, 3).wait()
+
+    def step(i, carry):
+        s, m = i // chunks + 1, lax.rem(i, chunks)
+        low, high = at - s, at + s
+
+        @pl.when(low >= 0)
+        def _():
+            pass_on(low, m, 0, s).wait_recv()
+
+            @pl.when(has_right)
+            def _():
+                pass_on(low, m, 0, s).start()
+
+        @pl.when(high < n)
+        def _():
+            pass_on(high, m, 1, s).wait_recv()
+
+            @pl.when(has_left)
+            def _():
+                pass_on(high, m, 1, s).start()
+
+        @pl.when(low >= 0)
+        def _():
+            multiply(low, m, False)
+
+        @pl.when(high < n)
+        def _():
+            multiply(high, m, False)
+
+        return carry
+
+    lax.fori_loop(0, (n - 1) * chunks, step, 0)
+
+    def drain(i, carry):
+        s, m = i // chunks, lax.rem(i, chunks)
+
+        @pl.when((at - s >= 0) & has_right)
+        def _():
+            pass_on(at - s, m, 0, s).wait_send()
+
+        @pl.when((at + s < n) & has_left)
+        def _():
+            pass_on(at + s, m, 1, s).wait_send()
+
+        return carry
+
+    lax.fori_loop(0, n * chunks, drain, 0)
 
     for d in range(1, sections):
         to = peer(d)
@@ -298,7 +438,7 @@
     return out.reshape(chunks * chunk, columns)
 
 
-def retain(q, k, v, log_decay, prompt_section, q_step, k_step, v_step, step_decay):
+def fused(q, k, v, log_decay, prompt_section, q_step, k_step, v_step, step_decay, w_out):
     tokens, heads, hd = q.shape
     rows, steps = q_step.shape[:2]
     sections = lax.axis_size("ctx")
@@ -314,7 +454,10 @@
     row_step = jnp.repeat(jnp.arange(steps), rows)
     pack = (slot[:, None] == row_slot[None, :]) & (slot_step[:, None] == row_step[None, :])
     unpack = (row_slot[:, None] == slot[None, :]) & (row_step[:, None] == slot_step[None, :])
-    step_logs = jnp.cumsum(step_decay, axis=1)
+    running = [step_decay[:, 0]]
+    for t in range(1, steps):
+        running.append(running[-1] + step_decay[:, t])
+    step_logs = jnp.stack(running, axis=1)
     step_logs = jnp.transpose(step_logs, (2, 1, 0)).reshape(rows, steps * heads)
 
     def wide(a):
@@ -323,29 +466,40 @@
     def by_step(a):
         return jnp.transpose(a, (1, 0, 2, 3)).reshape(steps * rows, heads * hd)
 
+    n = lax.axis_size("head")
+    chunk = rows * steps
+    chunks, depth = tokens // chunk + 1, heads * hd
     vmem = pl.BlockSpec(memory_space=pltpu.VMEM)
     count = sections * CAP * steps
     state = pltpu.VMEM((sections, hd, hd), BF16)
     reads = pltpu.VMEM((sections, count, hd), BF16)
     return pl.pallas_call(
-        functools.partial(retention_kernel, sections),
-        out_shape=jax.ShapeDtypeStruct((tokens + rows * steps, heads * hd), BF16),
-        in_specs=[vmem] * 12,
-        out_specs=vmem,
+        functools.partial(fused_kernel, sections),
+        out_shape=(
+            jax.ShapeDtypeStruct((tokens, depth), BF16),
+            jax.ShapeDtypeStruct((rows * steps, depth), BF16),
+        ),
+        in_specs=[vmem] * 12 + [pl.BlockSpec(memory_space=pl.ANY)],
+        out_specs=(vmem, vmem),
         scratch_shapes=[
             state, reads, state, reads, pltpu.VMEM((sections, 8, 128), F32),
             state, state, reads, state, reads,
-            pltpu.VMEM((tokens, heads * hd), F32),
-            pltpu.VMEM((rows * steps, heads * hd), F32),
-        ] + [pltpu.SemaphoreType.DMA((sections,))] * 10,
+            pltpu.VMEM((n, chunks, chunk, depth), BF16),
+            pltpu.VMEM((3, depth, depth), BF16),
+            pltpu.VMEM((chunks, chunk, depth), F32),
+        ] + [pltpu.SemaphoreType.DMA((sections,))] * 10 + [
+            pltpu.SemaphoreType.DMA((4,)),
+            pltpu.SemaphoreType.DMA((2, n, chunks)),
+            pltpu.SemaphoreType.DMA((n, chunks)),
+        ],
         compiler_params=pltpu.CompilerParams(
-            collective_id=0, has_side_effects=True, vmem_limit_bytes=48 * 2**20
+            collective_id=0, has_side_effects=True, vmem_limit_bytes=62 * 2**20
         ),
-        name="retain",
+        name="fused",
     )(
         wide(q), wide(k), wide(v), cumlog, cumlog.T, totals,
         by_step(q_step), by_step(k_step), by_step(v_step), step_logs,
-        pack.astype(BF16), unpack.astype(BF16),
+        pack.astype(BF16), unpack.astype(BF16), w_out,
     )
 
 
@@ -495,13 +649,17 @@
 ):
     tokens, heads = q_prompt.shape[:2]
     rows, steps = q_step.shape[:2]
-    form = retain if heads == lax.axis_size("ctx") else retain_gathered
-    flat = form(
+    sections, n = lax.axis_size("ctx"), lax.axis_size("head")
+    args = (
         q_prompt, k_prompt, v_prompt, log_decay, prompt_section, q_step, k_step, v_step, step_decay
     )
-    out = project(flat, w_out)
-    step_out = out[tokens:].reshape(steps, rows, w_out.shape[1])
-    return (out[:tokens], jnp.transpose(step_out, (1, 0, 2)))
+    if heads == sections and n == 4 and tokens % (rows * steps) == 0:
+        prompt_out, step_out = fused(*args, w_out)
+    else:
+        out = project(retain_gathered(*args), w_out)
+        prompt_out, step_out = out[:tokens], out[tokens:]
+    step_out = step_out.reshape(steps, rows, w_out.shape[1])
+    return (prompt_out, jnp.transpose(step_out, (1, 0, 2)))
 
 
 def solution(mesh):

time: 242 us -> 237 us (0.979)
  Pallas kernels: 223 us -> 210 us
  local copies, waits for them, and re-layouts: 13.3 us -> 19.1 us
    pallas_call x2 -> x1, Pallas kernels: 223 us -> 210 us  [fused(): pl.pallas_call(functools.partial(fused_kernel, sections), out_shape=(jax....]
    unnamed x16 -> x19, local copies, waits for them, and re-layouts: 6.76 us -> 12 us
where the time goes in v2:
time: 237 us; the launch traced here: 235 us
  Pallas kernels  210 us (89%)
  local copies, waits for them, and re-layouts  19.1 us (8%)
  other arithmetic  4.75 us (2%)
    pallas_call x1, Pallas kernels, fused(): pl.pallas_call(functools.partial(fused_kernel, sections), out_shape=(jax....  210 us
    unnamed x19, local copies, waits for them, and re-layouts  12 us

profile of v2, /device:TPU:0, one launch (start us, length us, event | category | flops | bytes accessed | tf_op | source)
XLA Modules:
  0.0 234.5 jit_solution(6602649330579026829)
XLA Ops:
  0.6 0.0 copy-start.4
  0.7 0.9 select_reduce_fusion
  1.6 0.7 multiply_add_fusion
  2.2 0.1 eq.84
  2.3 0.1 eq.89
  2.4 0.1 iota_add_fusion
  2.5 0.1 eq.79
  2.6 2.2 reduce-window.6
  4.8 0.2 slice_reduce_fusion
  5.0 0.1 broadcast_add_fusion
  5.1 0.1 eq.87
  5.2 0.9 fusion.2
  6.1 0.7 copy.39.step_log_ref
  6.8 0.8 and_convert_fusion
  7.6 0.1 copy.30
  7.7 0.0 copy-start
  7.7 0.7 copy.38.cum_ref
  8.4 0.7 broadcast_in_dim.42.total_ref
  9.1 0.0 copy-start.5
  9.1 1.1 copy.31
  10.2 0.9 copy.48
  11.2 0.0 copy-done.4
  11.2 0.0 copy-start.1
  11.2 0.9 copy.49
  12.1 0.0 copy-done
  12.1 0.0 copy-done.5
  12.2 0.9 copy.50
  13.1 0.0 copy-done.1
  13.1 0.0 copy-start.2
  13.1 2.0 copy.45
  15.1 0.0 copy-done.2
  15.1 0.0 copy-start.3
  15.1 2.0 copy.46
  17.2 0.0 copy-done.3
  17.2 2.0 copy.47
  19.1 210.0 %fused.1 = (bf16[512,2048]{1,0:T(8,128)(2,1)}, bf16[128,2048]{1,0:T(8,128)(2,1)}) custom-call(bf16[512,2048]{1,0:T(8,128)(2,1)} %bitcast.38, bf16[512,2048]{1,0:T(8,128)(2,1)} %bitcast.39, bf16[512,2048]{1,0:T(8,128)(2,1)} %bitcast.40, f32[8,512]{1,0:T(8,128)} %copy.38.cum_ref, f32[512,8]{1,0:T(8,128)} %bitcast.43, f32[8,8,128]{2,1,0:T(8,128)} %broadcast_in_dim.42.total_ref, ...), custom_call_target="tpu_custom_call" | custom-call | tf_op jit(solution)/shard_map/fused/pallas_call | solution.py:476
  229.1 2.2 copy.52
  231.4 3.2 %copy.54 = bf16[512,2048]{1,0:T(8,128)(2,1)} copy(bf16[512,2048]{1,0:T(8,128)(2,1)} %get-tuple-element.17) | data formatting | bytes 4194304
  (13 shorter events, 0.2 us)
Async XLA Ops:
  0.6 10.5 %copy-start.4 = (bf16[32,4,8,256]{3,2,1,0:T(8,128)(2,1)S(1)}, bf16[32,4,8,256]{3,2,1,0:T(8,128)(2,1)}, u32[]{:S(2)}) copy-start(bf16[32,4,8,256]{3,2,1,0:T(8,128)(2,1)} %param.16) | copy-start | bytes 1572868
  7.7 4.4 %copy-start = (f32[8,4,128]{0,2,1:T(8,128)}, f32[8,4,128]{0,2,1:T(8,128)S(1)}, u32[]{:S(2)}) copy-start(f32[8,4,128]{0,2,1:T(8,128)S(1)} %copy.30) | copy-start | bytes 49156
  9.1 3.0 %copy-start.5 = (bf16[32,4,8,256]{3,2,1,0:T(8,128)(2,1)S(1)}, bf16[32,4,8,256]{3,2,1,0:T(8,128)(2,1)}, u32[]{:S(2)}) copy-start(bf16[32,4,8,256]{3,2,1,0:T(8,128)(2,1)} %param.17) | copy-start | bytes 1572868
  11.2 1.9 copy-start.1
  13.1 2.0 copy-start.2
  15.1 2.0 copy-start.3

commit v3 on v2

--- a/solution.py
+++ b/solution.py
@@ -18,11 +18,12 @@
 
 def fused_kernel(
     sections,
-    q_ref, k_ref, v_ref, cum_ref, cum_t_ref, total_ref,
-    qs_ref, ks_ref, vs_ref, step_log_ref, pack_ref, unpack_ref,
+    q_ref, k_ref, v_ref, decay_ref, section_ref,
+    qs_ref, ks_ref, vs_ref, step_decay_ref,
     w_ref,
     prompt_ref, step_ref,
-    state_out, query_out, state_in, query_in, total_in,
+    cum_ref, cum_t_ref, total_ref, step_log_ref, pack_ref,
+    step_part, state_out, query_out, state_in, query_in, total_in,
     boundary, entry_out, read_out, entry_in, read_in, gathered, weights, total,
     send_s, send_a, send_q, send_e, send_r,
     recv_s, recv_a, recv_q, recv_e, recv_r,
@@ -62,10 +63,10 @@
         @pl.when(has_left)
         def _():
             pass_on(at, m, 1, 0).start()
-    heads = total_ref.shape[0]
+    heads = decay_ref.shape[0]
     tokens = q_ref.shape[0]
     hd = q_ref.shape[1] // heads
-    rows = step_log_ref.shape[0]
+    rows = section_ref.shape[0]
     steps = qs_ref.shape[0] // rows
 
     def peer(d):
@@ -96,6 +97,21 @@
 
     def lanes(h):
         return slice(h * hd, (h + 1) * hd)
+
+    def iota(shape, axis):
+        return lax.broadcasted_iota(jnp.int32, shape, axis)
+
+    def exact(a, b, dims):
+        return lax.dot_general(
+            a, b, (dims, ((), ())), precision=lax.Precision.HIGHEST, preferred_element_type=F32
+        )
+
+    causal = iota((tokens, tokens), 0) >= iota((tokens, tokens), 1)
+    ones = causal.astype(F32)
+    cum_ref[...] = exact(decay_ref[...], ones, ((1,), (1,)))
+    cum_t_ref[...] = exact(ones, decay_ref[...], ((1,), (1,)))
+    for h in range(heads):
+        total_ref[h] = jnp.broadcast_to(cum_t_ref[tokens - 1:tokens, h:h + 1], (8, 128))
 
     for h in range(heads):
         column = cum_t_ref[:, h:h + 1]
@@ -113,17 +129,6 @@
     state_in[me] = state_out[me]
     total_in[me] = total_ref[me]
     for h in range(heads):
-        query_out[h] = mm(pack_ref[...], qs_ref[:, lanes(h)]).astype(BF16)
-    for d in range(1, sections):
-        to = peer(d)
-        push(query_out.at[to], query_in.at[me], send_q.at[d], recv_q.at[me], to).start()
-    query_in[me] = query_out[me]
-
-    causal = (
-        lax.broadcasted_iota(jnp.int32, (tokens, tokens), 0)
-        >= lax.broadcasted_iota(jnp.int32, (tokens, tokens), 1)
-    )
-    for h in range(heads):
         scores = lax.dot_general(
             q_ref[:, lanes(h)], k_ref[:, lanes(h)], (((1,), (1,)), ((), ())),
             preferred_element_type=F32,
@@ -131,6 +136,27 @@
         gap = jnp.minimum(cum_t_ref[:, h:h + 1] - cum_ref[h:h + 1, :], 0.0)
         scaled = jnp.where(causal, scores * jnp.exp(gap), 0.0).astype(BF16)
         total[0:parts, :, lanes(h)] = mm(scaled, v_ref[:, lanes(h)]).reshape(parts, chunk, hd)
+
+    square = (rows, rows)
+    section = jnp.broadcast_to(section_ref[...], square)
+    across = jnp.sum(jnp.where(iota(square, 0) == iota(square, 1), section, 0), axis=0, keepdims=True)
+    earlier = (section == across) & (iota(square, 0) < iota(square, 1))
+    ranking = jnp.sum(jnp.where(earlier, 1, 0), axis=0, keepdims=True)
+    span = CAP * steps
+    base = (iota((sections * CAP, rows), 0) == across * CAP + ranking).astype(BF16)
+    wide = (sections * span, sections * CAP)
+    spread = (iota(wide, 0) // span == iota(wide, 1) // CAP) & (iota(wide, 0) % CAP == iota(wide, 1) % CAP)
+    tall = (rows, rows * steps)
+    repeat = (iota(tall, 1) % rows == iota(tall, 0)).astype(BF16)
+    full = (sections * span, rows * steps)
+    pack = mm(mm(spread.astype(BF16), base).astype(BF16), repeat)
+    same_step = iota(full, 0) % span // CAP == iota(full, 1) // rows
+    pack_ref[...] = jnp.where(same_step, pack, 0.0).astype(BF16)
+    tied = (heads * steps, heads * steps)
+    summed = (iota(tied, 0) // steps == iota(tied, 1) % heads) & (iota(tied, 0) % steps <= iota(tied, 1) // heads)
+    step_log_ref[...] = exact(step_decay_ref[...], summed.astype(F32), ((0,), (0,)))
+    for h in range(heads):
+        query_out[h] = mm(pack_ref[...], qs_ref[:, lanes(h)]).astype(BF16)
 
     for d in range(1, sections):
         frm = peer(d)
@@ -145,19 +171,6 @@
         to = peer(d)
         push(entry_out.at[to], entry_in.at[me], send_e.at[d], recv_e.at[me], to).start()
     entry_in[me] = entry_out[me]
-
-    for d in range(1, sections):
-        frm = peer(d)
-        push(query_out.at[frm], query_in.at[frm], send_q.at[d], recv_q.at[frm], frm).wait_recv()
-    span = CAP * steps
-    for c in range(sections):
-        part = slice(c * span, (c + 1) * span)
-        asked = query_in[:, part, :].reshape(sections * span, hd)
-        read_out[:, part, :] = mm(asked, boundary[c]).astype(BF16).reshape(sections, span, hd)
-    for d in range(1, sections):
-        to = peer(d)
-        push(read_out.at[to], read_in.at[me], send_r.at[d], recv_r.at[me], to).start()
-    read_in[me] = read_out[me]
 
     for h in range(heads):
         for t in range(steps):
@@ -184,17 +197,9 @@
         send_own(m)
 
     for d in range(1, sections):
-        frm = peer(d)
-        push(read_out.at[frm], read_in.at[frm], send_r.at[d], recv_r.at[frm], frm).wait_recv()
-    for h in range(heads):
-        reads = mm(unpack_ref[...], read_in[h])
-        for t in range(steps):
-            here = slice(t * rows, (t + 1) * rows)
-            grown = jnp.exp(step_log_ref[:, t * heads + h:t * heads + h + 1])
-            gathered[at, parts, here, lanes(h)] = (
-                grown * reads[here] + total[parts, here, lanes(h)]
-            ).astype(BF16)
-    send_own(parts)
+        to = peer(d)
+        push(query_out.at[to], query_in.at[me], send_q.at[d], recv_q.at[me], to).start()
+    query_in[me] = query_out[me]
 
     def multiply(j, m, first):
         slot = slot_of(j)
@@ -223,13 +228,46 @@
 
         lax.fori_loop(0, depth // tile, body, 0)
 
-    load(at, 0).wait()
-
     def own_step(m, carry):
         multiply(at, m, True)
         return carry
 
-    lax.fori_loop(0, chunks, own_step, 0)
+    load(at, 0).wait()
+    lax.fori_loop(0, parts // 2, own_step, 0)
+
+    for d in range(1, sections):
+        frm = peer(d)
+        push(query_out.at[frm], query_in.at[frm], send_q.at[d], recv_q.at[frm], frm).wait_recv()
+    for c in range(sections):
+        part = slice(c * span, (c + 1) * span)
+        asked = query_in[:, part, :].reshape(sections * span, hd)
+        read_out[:, part, :] = mm(asked, boundary[c]).astype(BF16).reshape(sections, span, hd)
+    for d in range(1, sections):
+        to = peer(d)
+        push(read_out.at[to], read_in.at[me], send_r.at[d], recv_r.at[me], to).start()
+    read_in[me] = read_out[me]
+
+    lax.fori_loop(parts // 2, parts, own_step, 0)
+
+    for d in range(1, sections):
+        frm = peer(d)
+        push(read_out.at[frm], read_in.at[frm], send_r.at[d], recv_r.at[frm], frm).wait_recv()
+    line = (rows * steps, rows * steps)
+    order = (iota(line, 1) == iota(line, 0) % steps * rows + iota(line, 0) // steps).astype(BF16)
+    for h in range(heads):
+        reads = lax.dot_general(
+            pack_ref[...], read_in[h], (((0,), (0,)), ((), ())), preferred_element_type=F32
+        )
+        for t in range(steps):
+            here = slice(t * rows, (t + 1) * rows)
+            grown = jnp.exp(step_log_ref[:, t * heads + h:t * heads + h + 1])
+            step_part[here] = (
+                grown * reads[here] + total[parts, here, lanes(h)]
+            ).astype(BF16)
+        gathered[at, parts, :, lanes(h)] = mm(order, step_part[...]).astype(BF16)
+    send_own(parts)
+
+    multiply(at, parts, True)
     load(far, 3).start()
     load(near, 1).wait()
     load(other, 2).wait()
@@ -442,24 +480,6 @@
     tokens, heads, hd = q.shape
     rows, steps = q_step.shape[:2]
     sections = lax.axis_size("ctx")
-    cumlog = jnp.cumsum(log_decay, axis=1)
-    totals = jnp.broadcast_to(cumlog[:, -1][:, None, None], (heads, 8, 128))
-    section_ids = prompt_section[:, 0]
-    same = section_ids[:, None] == section_ids[None, :]
-    ranking = jnp.sum(jnp.where(jnp.tril(same, -1), 1, 0), axis=1)
-    slot = (jnp.arange(sections)[:, None, None] * CAP + jnp.arange(CAP)[None, None, :])
-    slot = jnp.broadcast_to(slot, (sections, steps, CAP)).reshape(-1)
-    slot_step = jnp.broadcast_to(jnp.arange(steps)[None, :, None], (sections, steps, CAP)).reshape(-1)
-    row_slot = jnp.tile(section_ids * CAP + ranking, steps)
-    row_step = jnp.repeat(jnp.arange(steps), rows)
-    pack = (slot[:, None] == row_slot[None, :]) & (slot_step[:, None] == row_step[None, :])
-    unpack = (row_slot[:, None] == slot[None, :]) & (row_step[:, None] == slot_step[None, :])
-    running = [step_decay[:, 0]]
-    for t in range(1, steps):
-        running.append(running[-1] + step_decay[:, t])
-    step_logs = jnp.stack(running, axis=1)
-    step_logs = jnp.transpose(step_logs, (2, 1, 0)).reshape(rows, steps * heads)
-
     def wide(a):
         return a.reshape(tokens, heads * hd)
 
@@ -479,9 +499,15 @@
             jax.ShapeDtypeStruct((tokens, depth), BF16),
             jax.ShapeDtypeStruct((rows * steps, depth), BF16),
         ),
-        in_specs=[vmem] * 12 + [pl.BlockSpec(memory_space=pl.ANY)],
+        in_specs=[vmem] * 9 + [pl.BlockSpec(memory_space=pl.ANY)],
         out_specs=(vmem, vmem),
         scratch_shapes=[
+            pltpu.VMEM((heads, tokens), F32),
+            pltpu.VMEM((tokens, heads), F32),
+            pltpu.VMEM((heads, 8, 128), F32),
+            pltpu.VMEM((rows, heads * steps), F32),
+            pltpu.VMEM((count, rows * steps), BF16),
+            pltpu.VMEM((rows * steps, hd), BF16),
             state, reads, state, reads, pltpu.VMEM((sections, 8, 128), F32),
             state, state, reads, state, reads,
             pltpu.VMEM((n, chunks, chunk, depth), BF16),
@@ -497,9 +523,9 @@
         ),
         name="fused",
     )(
-        wide(q), wide(k), wide(v), cumlog, cumlog.T, totals,
-        by_step(q_step), by_step(k_step), by_step(v_step), step_logs,
-        pack.astype(BF16), unpack.astype(BF16), w_out,
+        wide(q), wide(k), wide(v), log_decay, prompt_section,
+        by_step(q_step), by_step(k_step), by_step(v_step),
+        step_decay.reshape(heads * steps, rows), w_out,
     )
 
 
@@ -655,11 +681,10 @@
     )
     if heads == sections and n == 4 and tokens % (rows * steps) == 0:
         prompt_out, step_out = fused(*args, w_out)
-    else:
-        out = project(retain_gathered(*args), w_out)
-        prompt_out, step_out = out[:tokens], out[tokens:]
-    step_out = step_out.reshape(steps, rows, w_out.shape[1])
-    return (prompt_out, jnp.transpose(step_out, (1, 0, 2)))
+        return (prompt_out, step_out.reshape(rows, steps, w_out.shape[1]))
+    out = project(retain_gathered(*args), w_out)
+    step_out = out[tokens:].reshape(steps, rows, w_out.shape[1])
+    return (out[:tokens], jnp.transpose(step_out, (1, 0, 2)))
 
 
 def solution(mesh):

time: 237 us -> 228 us (0.962)
  other arithmetic: 4.75 us -> 0 us
  local copies, waits for them, and re-layouts: 19.1 us -> 16.6 us
    unnamed x19 -> x18, local copies, waits for them, and re-layouts: 12 us -> 13.3 us
where the time goes in v3:
time: 228 us; the launch traced here: 227 us
  Pallas kernels  210 us (92%)
  local copies, waits for them, and re-layouts  16.6 us (7%)
    pallas_call x1, Pallas kernels, fused(): pl.pallas_call(functools.partial(fused_kernel, sections), out_shape=(jax....  210 us
    unnamed x18, local copies, waits for them, and re-layouts  13.3 us

profile of v3, /device:TPU:0, one launch (start us, length us, event | category | flops | bytes accessed | tf_op | source)
XLA Modules:
  0.0 227.4 jit_solution(8141812035744900674)
XLA Ops:
  0.6 0.0 copy-start.3
  0.6 1.4 copy.15.section_ref
  2.0 0.0 copy-start.4
  2.0 1.1 copy.12
  3.2 0.9 copy.19
  4.1 0.0 copy-done.3
  4.1 0.0 copy-start
  4.1 0.9 copy.20
  5.0 0.0 copy-done.4
  5.1 0.9 copy.21
  6.0 0.0 copy-done
  6.0 0.0 copy-start.1
  6.0 2.0 copy.16
  8.0 0.0 copy-done.1
  8.0 0.0 copy-start.2
  8.0 2.0 copy.17
  10.0 0.0 copy-done.2
  10.0 2.0 copy.18
  12.0 210.2 %fused.1 = (bf16[512,2048]{1,0:T(8,128)(2,1)}, bf16[128,2048]{1,0:T(8,128)(2,1)}) custom-call(bf16[512,2048]{1,0:T(8,128)(2,1)} %bitcast.19, bf16[512,2048]{1,0:T(8,128)(2,1)} %bitcast.20, bf16[512,2048]{1,0:T(8,128)(2,1)} %bitcast.21, f32[8,512]{1,0:T(8,128)} %decay_ref.1, s32[32,1]{1,0:T(8,128)} %copy.15.section_ref, bf16[128,2048]{1,0:T(8,128)(2,1)} %bitcast.22, ...), custom_call_target="tpu_custom_call" | custom-call | tf_op jit(solution)/shard_map/fused/pallas_call | solution.py:496
  222.2 2.0 reshape.35
  224.2 3.2 %copy.23 = bf16[512,2048]{1,0:T(8,128)(2,1)} copy(bf16[512,2048]{1,0:T(8,128)(2,1)} %get-tuple-element.8) | data formatting | bytes 4194304
  (2 shorter events, 0.1 us)
Async XLA Ops:
  0.6 3.5 %copy-start.3 = (bf16[32,4,8,256]{3,2,1,0:T(8,128)(2,1)S(1)}, bf16[32,4,8,256]{3,2,1,0:T(8,128)(2,1)}, u32[]{:S(2)}) copy-start(bf16[32,4,8,256]{3,2,1,0:T(8,128)(2,1)} %param.16) | copy-start | bytes 1572868
  2.0 3.0 %copy-start.4 = (bf16[32,4,8,256]{3,2,1,0:T(8,128)(2,1)S(1)}, bf16[32,4,8,256]{3,2,1,0:T(8,128)(2,1)}, u32[]{:S(2)}) copy-start(bf16[32,4,8,256]{3,2,1,0:T(8,128)(2,1)} %param.17) | copy-start | bytes 1572868
  4.1 1.9 copy-start
  6.0 2.0 copy-start.1
  8.0 2.0 copy-start.2

commit v4 on v3

--- a/solution.py
+++ b/solution.py
@@ -108,7 +108,6 @@
 
     causal = iota((tokens, tokens), 0) >= iota((tokens, tokens), 1)
     ones = causal.astype(F32)
-    cum_ref[...] = exact(decay_ref[...], ones, ((1,), (1,)))
     cum_t_ref[...] = exact(ones, decay_ref[...], ((1,), (1,)))
     for h in range(heads):
         total_ref[h] = jnp.broadcast_to(cum_t_ref[tokens - 1:tokens, h:h + 1], (8, 128))
@@ -128,6 +127,7 @@
         push(state_out.at[to], state_in.at[me], send_s.at[d], recv_s.at[me], to).start()
     state_in[me] = state_out[me]
     total_in[me] = total_ref[me]
+    cum_ref[...] = exact(decay_ref[...], ones, ((1,), (1,)))
     for h in range(heads):
         scores = lax.dot_general(
             q_ref[:, lanes(h)], k_ref[:, lanes(h)], (((1,), (1,)), ((), ())),
@@ -167,9 +167,12 @@
         entry_out[c] = state.astype(BF16)
         state = jnp.exp(total_in[c, 0:1, 0:1]) * state + state_in[c].astype(F32)
         boundary[c] = state.astype(BF16)
-    for d in range(1, sections):
-        to = peer(d)
-        push(entry_out.at[to], entry_in.at[me], send_e.at[d], recv_e.at[me], to).start()
+
+        @pl.when(me != c)
+        def _():
+            gap = lax.rem(c - me + sections, sections)
+            push(entry_out.at[c], entry_in.at[me], send_e.at[gap], recv_e.at[me], c).start()
+
     entry_in[me] = entry_out[me]
 
     for h in range(heads):

time: 228 us -> 226 us (level)
  Pallas kernels: 210 us -> 207 us
    pallas_call x1, Pallas kernels: 210 us -> 207 us  [fused(): pl.pallas_call(functools.partial(fused_kernel, sections), out_shape=(jax....]
where the time goes in v4:
time: 226 us; the launch traced here: 224 us
  Pallas kernels  207 us (92%)
  local copies, waits for them, and re-layouts  16.6 us (7%)
    pallas_call x1, Pallas kernels, fused(): pl.pallas_call(functools.partial(fused_kernel, sections), out_shape=(jax....  207 us
    unnamed x18, local copies, waits for them, and re-layouts  13.3 us

profile of v4, /device:TPU:0, one launch (start us, length us, event | category | flops | bytes accessed | tf_op | source)
XLA Modules:
  0.0 224.0 jit_solution(1570735762353561357)
XLA Ops:
  0.6 0.0 copy-start.3
  0.6 1.4 copy.15.section_ref
  2.0 0.0 copy-start.4
  2.0 1.1 copy.12
  3.2 0.9 copy.19
  4.1 0.0 copy-done.3
  4.1 0.0 copy-start
  4.1 0.9 copy.20
  5.0 0.0 copy-done.4
  5.1 0.9 copy.21
  6.0 0.0 copy-done
  6.0 0.0 copy-start.1
  6.0 2.0 copy.16
  8.0 0.0 copy-done.1
  8.0 0.0 copy-start.2
  8.0 2.0 copy.17
  10.0 0.0 copy-done.2
  10.0 2.0 copy.18
  12.0 206.7 %fused.1 = (bf16[512,2048]{1,0:T(8,128)(2,1)}, bf16[128,2048]{1,0:T(8,128)(2,1)}) custom-call(bf16[512,2048]{1,0:T(8,128)(2,1)} %bitcast.19, bf16[512,2048]{1,0:T(8,128)(2,1)} %bitcast.20, bf16[512,2048]{1,0:T(8,128)(2,1)} %bitcast.21, f32[8,512]{1,0:T(8,128)} %decay_ref.1, s32[32,1]{1,0:T(8,128)} %copy.15.section_ref, bf16[128,2048]{1,0:T(8,128)(2,1)} %bitcast.22, ...), custom_call_target="tpu_custom_call" | custom-call | tf_op jit(solution)/shard_map/fused/pallas_call | solution.py:499
  218.8 2.0 reshape.35
  220.8 3.2 %copy.23 = bf16[512,2048]{1,0:T(8,128)(2,1)} copy(bf16[512,2048]{1,0:T(8,128)(2,1)} %get-tuple-element.8) | data formatting | bytes 4194304
  (2 shorter events, 0.1 us)
Async XLA Ops:
  0.6 3.5 %copy-start.3 = (bf16[32,4,8,256]{3,2,1,0:T(8,128)(2,1)S(1)}, bf16[32,4,8,256]{3,2,1,0:T(8,128)(2,1)}, u32[]{:S(2)}) copy-start(bf16[32,4,8,256]{3,2,1,0:T(8,128)(2,1)} %param.16) | copy-start | bytes 1572868
  2.0 3.0 %copy-start.4 = (bf16[32,4,8,256]{3,2,1,0:T(8,128)(2,1)S(1)}, bf16[32,4,8,256]{3,2,1,0:T(8,128)(2,1)}, u32[]{:S(2)}) copy-start(bf16[32,4,8,256]{3,2,1,0:T(8,128)(2,1)} %param.17) | copy-start | bytes 1572868
  4.1 1.9 copy-start
  6.0 2.0 copy-start.1
  8.0 2.0 copy-start.2
